TPU v7x, 32 devices: a whole 2x2x4 slice. The times are simulated.
32 devices in a mesh: rep: 8 (over z, y), blk: 4 (over x, core).
Axes of the slice: x: 2, y: 2, z: 4, core: 2. Of those that a mesh axis runs over, the one named last changes fastest.
Arguments:
- encoded: bfloat16 [128, 512, 512], P(('rep', 'blk')), may hold values from -6 to 6
- queries: bfloat16 [1024, 512], P('blk'), may hold values from -0.25 to 0.25
- classifiers: bfloat16 [1024, 512], P('blk'), may hold values from -1 to 1
- lengths: int32 [128], P(('rep', 'blk')), may hold values from 1 to 512, 49152 in all
- beam: int32 [128, 1024], P(('rep', 'blk')), may hold values 0 or 1
- logit_grad: float32 [128, 1024], P(('rep', 'blk')), may hold values from -6 to 6
Outputs:
- logits: float32 [128, 1024], P(('rep', 'blk'))
- encoded_grad: bfloat16 [128, 512, 512], P(('rep', 'blk'))
- label_grad: float32 [1024, 1024], P('blk')
Inputs may be any that keep to these rules, and one draw needn't show every extreme that they name: `lengths`: every document has at least one real token, and some document has exactly 512.
All inputs are finite; a program needn't handle non-finite values. No bound on the sum of `lengths` or of `beam` on one device may be relied on, other than what follows from the above.
Results may differ from a plain program's by a relative error of at most 0.0058.
Values may be sent and summed in bfloat16 or wider, within the bound.
No kernel may reach another device: no remote copies, remote signals or barrier semaphores. Data moves between devices by JAX's collectives and lax.ppermute only.
A program may use at most 64 MiB of HBM per device.

v0:
```python
import functools

import jax
import jax.numpy as jnp
from jax import lax
from jax.experimental import pallas as pl
from jax.experimental.pallas import tpu as pltpu
from jax.sharding import PartitionSpec as P

F32 = jnp.float32
BF16 = jnp.bfloat16
VMEM = pl.BlockSpec(memory_space=pltpu.VMEM)
SMEM = pl.BlockSpec(memory_space=pltpu.SMEM)
HBM = pl.BlockSpec(memory_space=pltpu.HBM)
PARAMS = pltpu.CompilerParams(vmem_limit_bytes=20 * 1024 * 1024)
GROUP = 4
EXTRA = 16


def shape(dims, dtype):
    return jax.ShapeDtypeStruct(dims, dtype)


def mm(a, b):
    return jnp.dot(a, b, preferred_element_type=F32)


def cost(products, docs, tokens, width, labels):
    return pl.CostEstimate(
        flops=2 * products * docs * tokens * width * labels,
        transcendentals=docs * tokens * labels,
        bytes_accessed=4 * docs * tokens * width,
    )


def call(kernel, out_shape, ins, name, scratch=(), estimate=None, hbm=0):
    single = not isinstance(out_shape, (list, tuple))
    ins = [pltpu.with_memory_space_constraint(x, pltpu.HBM) for x in ins[:hbm]] + list(ins[hbm:])
    return pl.pallas_call(
        kernel,
        out_shape=out_shape,
        in_specs=[
            HBM if i < hbm else SMEM if x.ndim == 1 else VMEM for i, x in enumerate(ins)
        ],
        out_specs=VMEM if single else [VMEM] * len(out_shape),
        scratch_shapes=scratch,
        compiler_params=PARAMS,
        cost_estimate=estimate,
        name=name,
    )(*ins)


def lanes_of(info_ref, k, labels):
    return pl.ds(pl.multiple_of((info_ref[0] ^ k) * labels, labels), labels)


def label_chunk(docs, q, c, lanes, sums):
    qt = q.T
    ct = c.T.astype(F32)
    labels = q.shape[0]

    def products(doc):
        load, enc_ref, enct_ref, gate_ref = doc[:4]
        load()
        enc = enc_ref[...]
        g = gate_ref[:, lanes]
        both = mm(enc, jnp.concatenate([qt, (ct * g).astype(BF16)], axis=1))
        return g, both[:, :labels], both[:, labels:]

    query_grad, class_grad = sums
    ahead = products(docs[0])
    for i, (_, _, enct_ref, _, length, attn_ref, score_ref, logit_ref) in enumerate(docs):
        g, scores, attn_grad = ahead
        if i + 1 < len(docs):
            ahead = products(docs[i + 1])
        token = lax.broadcasted_iota(jnp.int32, scores.shape, 0)
        expo = jnp.where(token < length, jnp.exp(scores), 0.0)
        attn = expo * (1.0 / jnp.sum(expo, axis=0, keepdims=True))
        attn_b = attn.astype(BF16)
        attn_ref[...] = attn_b
        inner = jnp.sum(attn * attn_grad, axis=0, keepdims=True)
        score_grad = (attn * (attn_grad - inner)).astype(BF16)
        score_ref[...] = score_grad
        both = mm(enct_ref[...], jnp.concatenate([attn_b, score_grad], axis=1))
        context, part = both[:, :labels], both[:, labels:]
        query_grad = part if query_grad is None else query_grad + part
        logit_ref[...] = jnp.sum(context * ct, axis=0, keepdims=True)
        part = context * g
        class_grad = part if class_grad is None else class_grad + part
    return query_grad, class_grad


def doc_list(loads, enc_ref, enct_ref, gate_ref, lens_ref, attn_ref, score_ref, logit_ref):
    return [
        (loads[d], enc_ref.at[d], enct_ref.at[d], gate_ref.at[d : d + 1], lens_ref[d],
         attn_ref.at[d], score_ref.at[d], logit_ref.at[d : d + 1])
        for d in range(enc_ref.shape[0])
    ]


def turn_around(enc_ref, enct_ref, copies=None):
    def load(d):
        if copies is not None:
            copies[d].wait()
        enct_ref[d] = enc_ref[d].T

    return [functools.partial(load, d) for d in range(enc_ref.shape[0])]


def pack_kernel(q_in, c_in, qc_ref, sem):
    copies = [pltpu.make_async_copy(x, qc_ref.at[i], sem.at[i]) for i, x in enumerate((q_in, c_in))]
    for copy in copies:
        copy.start()
    for copy in copies:
        copy.wait()


def own_kernel(enc_in, beam_in, grad_in, info_ref, lens_ref, qc_ref, enc_ref, gate_ref, enct_ref,
               attn_ref, score_ref, logit_ref, qsum_ref, csum_ref, beam_ref, sem):
    docs = enc_ref.shape[0]
    small = [(beam_in, beam_ref), (grad_in, gate_ref)]
    small = [pltpu.make_async_copy(x, y, sem.at[docs + i]) for i, (x, y) in enumerate(small)]
    copies = [
        pltpu.make_async_copy(enc_in.at[d], enc_ref.at[d], sem.at[d]) for d in range(docs)
    ]
    for copy in copies[:1] + small + copies[1:]:
        copy.start()
    loads = turn_around(enc_ref, enct_ref, copies)

    def first_load():
        load()
        for copy in small:
            copy.wait()
        gate_ref[...] = gate_ref[...] * beam_ref[...].astype(F32)

    load, loads[0] = loads[0], first_load
    qsum_ref[...], csum_ref[...] = label_chunk(
        doc_list(loads, enc_ref, enct_ref, gate_ref, lens_ref, attn_ref, score_ref, logit_ref),
        qc_ref[0], qc_ref[1], lanes_of(info_ref, 0, qc_ref.shape[1]), (None, None),
    )


def to_blocks(info_ref, sums, rows_ref, out_refs):
    query_grad, class_grad = sums
    width = query_grad.shape[0]
    rows_ref[:, :width] = query_grad.T
    rows_ref[:, width:] = class_grad.T
    size = rows_ref.shape[0] // GROUP
    count = GROUP // len(out_refs)
    for i in range(GROUP):
        ref = out_refs[i // count]
        block = rows_ref[pl.ds(pl.multiple_of((info_ref[1] ^ i) * size, size), size), :]
        ref[(i % count) * size : (i % count + 1) * size, :] = block.astype(ref.dtype)


def other_kernel(info_ref, lens_ref, beam_ref, grad_ref, enc_ref, qc_ref, qsum_ref, csum_ref,
                 gate_ref, enct_ref, attn_ref, score_ref, logit_ref, *refs):
    gate_ref[...] = grad_ref[...] * beam_ref[...].astype(F32)
    sums = label_chunk(
        doc_list(turn_around(enc_ref, enct_ref), enc_ref, enct_ref, gate_ref, lens_ref,
                 attn_ref, score_ref, logit_ref),
        qc_ref[0], qc_ref[1], lanes_of(info_ref, 0, qc_ref.shape[1]),
        (qsum_ref[...], csum_ref[...]),
    )
    to_blocks(info_ref, sums, refs[-1], refs[:-1])


def far_kernel(info_ref, lens_ref, lens2_ref, gate_ref, gate2_ref, enc_ref, enc2_ref, enct_ref,
               enct2_ref, qc_ref, attn_ref, score_ref, logit_ref, attn2_ref, score2_ref,
               logit2_ref, *refs):
    loads = [lambda: None] * enc_ref.shape[0]
    sums = label_chunk(
        doc_list(loads, enc_ref, enct_ref, gate_ref, lens_ref, attn_ref, score_ref, logit_ref)
        + doc_list(loads, enc2_ref, enct2_ref, gate2_ref, lens2_ref, attn2_ref, score2_ref,
                   logit2_ref),
        qc_ref[0], qc_ref[1], lanes_of(info_ref, 2, qc_ref.shape[1]), (None, None),
    )
    to_blocks(info_ref, sums, refs[-1], refs[:-1])


def state_parts(ks, info_ref, gate_ref, chunks):
    docs, labels = gate_ref.shape[0], chunks[2].shape[1]
    ctx_grads = []
    for n, k in enumerate(ks):
        gate = gate_ref[:, lanes_of(info_ref, k, labels)]
        gate = jnp.concatenate([gate, jnp.zeros((128 - docs, labels), F32)], axis=0).T
        c = chunks[4 * n + 2][1].astype(F32)
        ctx_grads.append([(c * gate[:, d : d + 1]).astype(BF16) for d in range(docs)])
    for d in range(docs):
        total = None
        for n in range(len(ks)):
            attn_ref, score_ref, qc_ref = chunks[4 * n : 4 * n + 3]
            part = mm(attn_ref[d], ctx_grads[n][d]) + mm(score_ref[d], qc_ref[0])
            total = part if total is None else total + part
        yield d, total


def away_kernel(ks, info_ref, gate_ref, *refs):
    chunks, out_ref = refs[:-1], refs[-1]
    tokens, labels = chunks[0].shape[1:]
    for d, total in state_parts(ks, info_ref, gate_ref, chunks):
        out_ref[d, :tokens] = total.astype(BF16)
        for n in range(len(ks)):
            logit = chunks[4 * n + 3][d : d + 1, :]
            high = logit.astype(BF16).astype(F32)
            pad = jnp.zeros((EXTRA - 2, labels), F32)
            pair = jnp.concatenate([high, logit - high, pad], axis=0)
            out_ref[d, tokens:, n * labels : (n + 1) * labels] = pair.astype(BF16)


def home_kernel(ks, info_ref, gate_ref, *refs):
    chunks, (in_ref, out_ref, logit_ref, done_ref, sem) = refs[:-5], refs[-5:]
    tokens, labels = chunks[0].shape[1:]
    copies = []
    for d, total in state_parts(ks, info_ref, gate_ref, chunks):
        done_ref[d] = (total + in_ref[d, :tokens].astype(F32)).astype(BF16)
        copies.append(pltpu.make_async_copy(done_ref.at[d], out_ref.at[d], sem.at[d]))
        copies[-1].start()
        for n, k in enumerate(ks):
            pair = in_ref[d, tokens:, n * labels : (n + 1) * labels].astype(F32)
            logit_ref[d : d + 1, lanes_of(info_ref, k, labels)] = chunks[4 * n + 3][d : d + 1, :]
            logit_ref[d : d + 1, lanes_of(info_ref, k ^ 1, labels)] = pair[0:1] + pair[1:2]
    for copy in copies:
        copy.wait()


def state_grad(info, gate, parts, more):
    docs, tokens, labels = parts[0][0].shape
    width = parts[0][2].shape[2]
    ins = [info, gate, *parts[0], *parts[1], *more]
    estimate = cost(4, docs, tokens, width, labels)
    if not more:
        out = shape((docs, tokens + EXTRA, width), BF16)
        return call(functools.partial(away_kernel, (0, 2)), out, ins, "state_away", (), estimate)
    out = shape((docs, tokens, width), BF16)
    return pl.pallas_call(
        functools.partial(home_kernel, (0, 2)),
        out_shape=[out, shape(gate.shape, F32)],
        in_specs=[SMEM] + [VMEM] * (len(ins) - 1),
        out_specs=[pl.BlockSpec(memory_space=pl.ANY), VMEM],
        scratch_shapes=[pltpu.VMEM(out.shape, BF16), pltpu.SemaphoreType.DMA((docs,))],
        compiler_params=PARAMS,
        cost_estimate=estimate,
        name="state_home",
    )(*ins)


def add_kernel(count, *refs):
    total = refs[0][...].astype(F32)
    for ref in refs[1:count]:
        total = total + ref[...].astype(F32)
    size = refs[count].shape[0]
    for i, ref in enumerate(refs[count:]):
        ref[...] = total[i * size : (i + 1) * size].astype(ref.dtype)


def add(arrays, dtypes):
    rows, cols = arrays[0].shape
    out = [shape((rows // len(dtypes), cols), dtype) for dtype in dtypes]
    return call(functools.partial(add_kernel, len(arrays)), out, arrays, "add")


def rows_kernel(info_ref, *refs):
    block_refs, (out_ref, rows_ref, sem) = refs[:-3], refs[-3:]
    size = block_refs[0].shape[0]
    copies = []
    for i, ref in enumerate(block_refs):
        rows_ref[i] = ref[...].astype(F32)
        to = pl.ds(pl.multiple_of((info_ref[1] ^ i) * size, size), size)
        copies.append(pltpu.make_async_copy(rows_ref.at[i], out_ref.at[to], sem.at[i]))
        copies[-1].start()
    for copy in copies:
        copy.wait()


def to_rows(info, blocks):
    count = len(blocks)
    rows, cols = blocks[0].shape
    return pl.pallas_call(
        rows_kernel,
        out_shape=shape((count * rows, cols), F32),
        in_specs=[SMEM] + [VMEM] * count,
        out_specs=pl.BlockSpec(memory_space=pl.ANY),
        scratch_shapes=[pltpu.VMEM((count, rows, cols), F32), pltpu.SemaphoreType.DMA((count,))],
        compiler_params=PARAMS,
        name="to_rows",
    )(info, *blocks)


def per_device(reps, blks, encoded, queries, classifiers, lengths, beam, logit_grad):
    labels, width = queries.shape
    docs, tokens, _ = encoded.shape
    total = reps * blks
    blk, rep = lax.axis_index("blk"), lax.axis_index("rep")
    info = jnp.stack([blk, (rep & 1) * 2 + ((rep >> 1) & 1)]).astype(jnp.int32)

    def swap(x, mask):
        return lax.ppermute(x, ("rep", "blk"), [(i, i ^ mask) for i in range(total)])

    core, ax = 1, 2
    ay, az, azz = blks, 2 * blks, 4 * blks
    turns = [0, az, ay, ay | az]

    qc = call(
        pack_kernel, shape((2, labels, width), BF16), [queries, classifiers], "pack",
        [pltpu.SemaphoreType.DMA((2,))], hbm=2,
    )
    encoded2, qc = lax.optimization_barrier((encoded, qc))
    far_qc = swap(qc, ax)
    encoded2, beam2, grad2 = swap(encoded2, core), swap(beam, core), swap(logit_grad, core)
    lengths2 = swap(lengths, core)
    lengths = pltpu.with_memory_space_constraint(lengths, pltpu.HBM)

    per_chunk = [
        shape((docs, tokens, labels), BF16),
        shape((docs, tokens, labels), BF16),
        shape((docs, labels), F32),
    ]
    gates = shape(beam.shape, F32)
    turned = shape((docs, width, tokens), BF16)
    block = shape((labels // GROUP, 2 * width), BF16)
    halves = [shape((labels // 2, 2 * width), dtype) for dtype in (F32, BF16)]
    rows = [pltpu.VMEM((labels, 2 * width), F32)]
    sums = [shape((width, labels), F32)] * 2
    estimate = functools.partial(cost, tokens=tokens, width=width, labels=labels)

    enc, gate, enct, attn, score, logit, *acc = call(
        own_kernel,
        [shape(encoded.shape, BF16), gates, turned] + per_chunk + sums,
        [encoded, beam, logit_grad, info, lengths, qc], "own_labels",
        [pltpu.VMEM(beam.shape, jnp.int32), pltpu.SemaphoreType.DMA((docs + 2,))],
        estimate(4, docs), hbm=3,
    )
    gate2, enct2, attn2, score2, logit2, keep, send = call(
        other_kernel, [gates, turned] + per_chunk + halves,
        [info, lengths2, beam2, grad2, encoded2, qc, *acc], "own_labels_other_docs",
        rows, estimate(4, docs),
    )
    received = swap(send, ay)
    far_attn, far_score, far_logit, far_attn2, far_score2, far_logit2, *far = call(
        far_kernel, per_chunk + per_chunk + [shape(block.shape, F32)] + [block] * (GROUP - 1),
        [info, lengths, lengths2, gate, gate2, enc, encoded2, enct, enct2, far_qc],
        "far_labels", rows, estimate(4, 2 * docs),
    )

    far, keep, received = lax.optimization_barrier((far, keep, received))
    keep, send = add([keep, received], [F32, BF16])
    send, far = lax.optimization_barrier((send, far))
    relayed = swap(far[2], ay)
    received = [swap(far[3], ax | ay | az), swap(far[1], ax | az)]
    (first,) = add([far[0], relayed], [BF16])
    first, send, far_attn2 = lax.optimization_barrier((first, send, far_attn2))
    received.append(swap(first, ax))
    near = swap(send, az)
    state2 = state_grad(
        info, gate2,
        [(attn2, score2, qc, logit2), (far_attn2, far_score2, far_qc, far_logit2)], [],
    )
    received, state2, near = lax.optimization_barrier((received, state2, near))
    state_in = swap(state2, core)
    (own,) = add([keep, near, *received], [BF16])
    far_attn, far_score, own = lax.optimization_barrier((far_attn, far_score, own))
    state, logits = state_grad(
        info, gate, [(attn, score, qc, logit), (far_attn, far_score, far_qc, far_logit)],
        [state_in],
    )
    received, state = lax.optimization_barrier((swap(own, azz), state))
    (own,) = add([own, received], [BF16])
    if reps > 8:
        members = [[i * 8 + j for i in range(reps // 8)] for j in range(8)]
        own = lax.psum(own.astype(F32), "rep", axis_index_groups=members).astype(BF16)

    label_grad = to_rows(info, [own] + [swap(own, mask) for mask in turns[1:]])
    return logits, state, label_grad


def solution(mesh):
    reps, blks = mesh.shape["rep"], mesh.shape["blk"]
    assert blks == 4 and reps >= 8 and reps & (reps - 1) == 0
    in_specs = (
        P(("rep", "blk"), None, None),
        P("blk", None),
        P("blk", None),
        P(("rep", "blk")),
        P(("rep", "blk"), None),
        P(("rep", "blk"), None),
    )
    out_specs = (P(("rep", "blk"), None), P(("rep", "blk"), None, None), P("blk", None))
    return jax.shard_map(
        functools.partial(per_device, reps, blks),
        mesh=mesh, in_specs=in_specs, out_specs=out_specs, check_vma=False,
    )
```

profile of v0, /device:TPU:0, one launch (start us, length us, event | category | flops | bytes accessed | tf_op | source)
XLA Modules:
  0.0 58.0 jit_solution(6285435861858164882)
XLA Ops:
  0.6 1.0 %pack.1.qc_ref.refs_2_ = bf16[2,256,512]{2,1,0:T(8,128)(2,1)S(1)} custom-call(bf16[256,512]{1,0:T(8,128)(2,1)} %q_in.1, bf16[256,512]{1,0:T(8,128)(2,1)} %c_in.1), custom_call_target="tpu_custom_call" | custom-call | tf_op jit(solution)/shard_map/pack/pallas_call | solution.py:39
  1.7 0.5 collective-permute-start.3
  2.2 2.6 %collective-permute-start.4 = (bf16[2,256,512]{2,1,0:T(8,128)(2,1)S(1)}, bf16[2,256,512]{2,1,0:T(8,128)(2,1)S(1)}, u32[]{:S(2)}, u32[]{:S(2)}) collective-permute-start(bf16[2,256,512]{2,1,0:T(8,128)(2,1)S(1)} %pack.1.qc_ref.refs_2_), channel_id=1, source_target_pairs={{0,2},{1,3},{2,0},{3,1},{4,6},{5,7},{6,4},{7,5},{8,10},{9,11},{10,... | collective-permute-start | bytes 1572872 | tf_op jit(solution)/shard_map/ppermute | solution.py:298
  4.8 0.2 collective-permute-start
  4.9 0.3 collective-permute-start.1
  5.3 0.2 collective-permute-start.2
  5.4 0.1 pad_add_fusion.info_ref
  5.5 5.3 %own_labels.1 = (bf16[4,512,512]{2,1,0:T(8,128)(2,1)S(1)}, f32[4,1024]{1,0:T(4,128)S(1)}, bf16[4,512,512]{2,1,0:T(8,128)(2,1)S(1)}, bf16[4,512,256]{2,1,0:T(8,12...) custom-call(bf16[4,512,512]{2,1,0:T(8,128)(2,1)} %enc_in.1, ...), custom_call_target="tpu_custom_call" | custom-call | flops 2147483648 | bytes 4194304 | tf_op jit(solution)/shard_map/own_labels/pallas_call | solution.py:39
  10.8 0.0 collective-permute-done.lens_ref.lens2_ref
  10.8 0.0 collective-permute-done.1.beam_ref
  10.8 0.0 collective-permute-done.2.grad_ref
  10.8 0.0 collective-permute-done.3.enc_ref.enc2_ref
  10.9 3.6 %own_labels_other_docs.1 = (f32[4,1024]{1,0:T(4,128)S(1)}, bf16[4,512,512]{2,1,0:T(8,128)(2,1)S(1)}, bf16[4,512,256]{2,1,0:T(8,128)(2,1)S(1)}, bf16[4,512,256]{2...) custom-call(s32[2]{0:T(128)S(1)} %pad_add_fusion.info_ref, ...), custom_call_target="tpu_custom_call" | custom-call | flops 2147483648 | bytes 4194304 | tf_op jit(solution)/shard_map/own_labels_other_docs/pallas_call | solution.py:39
  14.5 1.6 %collective-permute-start.5 = (bf16[128,1024]{1,0:T(8,128)(2,1)S(1)}, bf16[128,1024]{1,0:T(8,128)(2,1)S(1)}, u32[]{:S(2)}, u32[]{:S(2)}) collective-permute-start(bf16[128,1024]{1,0:T(8,128)(2,1)S(1)} %get-tuple-element.77), channel_id=1, source_target_pairs={{0,4},{1,5},{2,6},{3,7},{4,0},{5,1},{6,2},{7,3},{8,12},{9,13},{10,... | collective-permute-start | bytes 786440 | tf_op jit(solution)/shard_map/ppermute | solution.py:298
  16.0 1.2 %collective-permute-done.4.qc_ref.refs_6_ = bf16[2,256,512]{2,1,0:T(8,128)(2,1)S(1)} collective-permute-done((bf16[2,256,512]{2,1,0:T(8,128)(2,1)S(1)}, bf16[2,256,512]{2,1,0:T(8,128)(2,1)S(1)}, u32[]{:S(2)}, u32[]{:S(2)}) %collective-permute-start.4) | collective-permute-done | bytes 524320 | tf_op jit(solution)/shard_map/ppermute | solution.py:298
  17.3 6.3 %far_labels.1 = (bf16[4,512,256]{2,1,0:T(8,128)(2,1)S(1)}, bf16[4,512,256]{2,1,0:T(8,128)(2,1)S(1)}, f32[4,256]{1,0:T(4,128)S(1)}, bf16[4,512,256]{2,1,0:T(8,128...) custom-call(s32[2]{0:T(128)S(1)} %pad_add_fusion.info_ref, ...), custom_call_target="tpu_custom_call" | custom-call | flops 4294967296 | bytes 8388608 | tf_op jit(solution)/shard_map/far_labels/pallas_call | solution.py:39
  23.6 0.0 collective-permute-done.5.refs_1_
  23.6 1.9 %collective-permute-start.8 = (bf16[64,1024]{1,0:T(8,128)(2,1)S(1)}, bf16[64,1024]{1,0:T(8,128)(2,1)S(1)}, u32[]{:S(2)}, u32[]{:S(2)}) collective-permute-start(bf16[64,1024]{1,0:T(8,128)(2,1)S(1)} %get-tuple-element.89), channel_id=1, source_target_pairs={{0,4},{1,5},{2,6},{3,7},{4,0},{5,1},{6,2},{7,3},{8,12},{9,13},{10,... | collective-permute-start | bytes 393224 | tf_op jit(solution)/shard_map/ppermute | solution.py:298
  25.5 2.5 %collective-permute-start.6 = (bf16[64,1024]{1,0:T(8,128)(2,1)S(1)}, bf16[64,1024]{1,0:T(8,128)(2,1)S(1)}, u32[]{:S(2)}, u32[]{:S(2)}) collective-permute-start(bf16[64,1024]{1,0:T(8,128)(2,1)S(1)} %get-tuple-element.86), channel_id=1, source_target_pairs={{0,14},{1,15},{2,12},{3,13},{4,10},{5,11},{6,8},{7,9},{8,6},{9,7},... | collective-permute-start | bytes 393224 | tf_op jit(solution)/shard_map/ppermute | solution.py:298
  28.0 0.1 collective-permute-start.7
  28.1 2.8 %collective-permute-done.8.refs_1_ = bf16[64,1024]{1,0:T(8,128)(2,1)S(1)} collective-permute-done((bf16[64,1024]{1,0:T(8,128)(2,1)S(1)}, bf16[64,1024]{1,0:T(8,128)(2,1)S(1)}, u32[]{:S(2)}, u32[]{:S(2)}) %collective-permute-start.8) | collective-permute-done | bytes 131104 | tf_op jit(solution)/shard_map/ppermute | solution.py:298
  31.0 0.4 collective-permute-start.9
  31.4 1.6 %collective-permute-start.10 = (bf16[64,1024]{1,0:T(8,128)(2,1)S(1)}, bf16[64,1024]{1,0:T(8,128)(2,1)S(1)}, u32[]{:S(2)}, u32[]{:S(2)}) collective-permute-start(bf16[64,1024]{1,0:T(8,128)(2,1)S(1)} %get-tuple-element.99), channel_id=1, source_target_pairs={{0,8},{1,9},{2,10},{3,11},{4,12},{5,13},{6,14},{7,15},{8,0},{9,1},... | collective-permute-start | bytes 393224 | tf_op jit(solution)/shard_map/ppermute | solution.py:298
  33.0 3.1 %state_away.1 = bf16[4,528,512]{2,1,0:T(8,128)(2,1)S(1)} custom-call(s32[2]{0:T(128)S(1)} %pad_add_fusion.info_ref, f32[4,1024]{1,0:T(4,128)S(1)} %get-tuple-element.66.gate2_ref.gate_ref, bf16[4,512,256]{2,1,0:T(8,128)(2,1)S(1)} %get-tuple-element.93.refs_0_, bf16[4,512,256]{2,1,0:T(8,128)(2,1)S(1)} %get-tuple-element.94.refs_1_, ...), custom_call_target="tpu_custom_call" | custom-call | flops 2147483648 | bytes 4194304 | tf_op jit(solution)/shard_map/state_away/pallas_call | solution.py:39
  36.0 0.0 collective-permute-done.6.refs_2_
  36.1 0.0 collective-permute-done.7.refs_3_
  36.1 0.6 %collective-permute-done.9.refs_4_ = bf16[64,1024]{1,0:T(8,128)(2,1)S(1)} collective-permute-done((bf16[64,1024]{1,0:T(8,128)(2,1)S(1)}, bf16[64,1024]{1,0:T(8,128)(2,1)S(1)}, u32[]{:S(2)}, u32[]{:S(2)}) %collective-permute-start.9) | collective-permute-done | bytes 131104 | tf_op jit(solution)/shard_map/ppermute | solution.py:298
  36.7 0.1 collective-permute-done.10.refs_1_
  36.9 0.0 collective-permute-start.11
  36.9 0.1 add.12.refs_0_
  37.0 2.7 %collective-permute-start.12 = (bf16[64,1024]{1,0:T(8,128)(2,1)S(1)}, bf16[64,1024]{1,0:T(8,128)(2,1)S(1)}, u32[]{:S(2)}, u32[]{:S(2)}) collective-permute-start(bf16[64,1024]{1,0:T(8,128)(2,1)S(1)} %add.12.refs_0_), channel_id=1, source_target_pairs={{0,16},{1,17},{2,18},{3,19},{4,20},{5,21},{6,22},{7,23},{8,24},{9,... | collective-permute-start | bytes 393224 | tf_op jit(solution)/shard_map/ppermute | solution.py:298
  39.7 1.4 %collective-permute-done.11.refs_8_ = bf16[4,528,512]{2,1,0:T(8,128)(2,1)S(1)} collective-permute-done((bf16[4,528,512]{2,1,0:T(8,128)(2,1)S(1)}, bf16[4,528,512]{2,1,0:T(8,128)(2,1)S(1)}, u32[]{:S(2)}, u32[]{:S(2)}) %collective-permute-start.11) | collective-permute-done | bytes 2162720 | tf_op jit(solution)/shard_map/ppermute | solution.py:298
  41.1 4.5 %state_home.1 = (bf16[4,512,512]{2,1,0:T(8,128)(2,1)}, f32[4,1024]{1,0:T(4,128)}) custom-call(s32[2]{0:T(128)S(1)} %pad_add_fusion.info_ref, f32[4,1024]{1,0:T(4,128)S(1)} %get-tuple-element.59.gate_ref, bf16[4,512,256]{2,1,0:T(8,128)(2,1)S(1)} %get-tuple-element.60.refs_0_, bf16[4,512,256]{2,1,0:T(8,128)(2,1)S(1)} %get-tuple-element.61.refs_1_, ...), custom_call_target="tpu_custom_call" | custom-call | flops 2147483648 | bytes 4194304 | tf_op jit(solution)/shard_map/state_home/pallas_call | solution.py:236
  45.7 1.0 %collective-permute-done.12.refs_1_ = bf16[64,1024]{1,0:T(8,128)(2,1)S(1)} collective-permute-done((bf16[64,1024]{1,0:T(8,128)(2,1)S(1)}, bf16[64,1024]{1,0:T(8,128)(2,1)S(1)}, u32[]{:S(2)}, u32[]{:S(2)}) %collective-permute-start.12) | collective-permute-done | bytes 131104 | tf_op jit(solution)/shard_map/ppermute | solution.py:298
  46.7 2.3 %collective-permute-start.15 = (bf16[64,1024]{1,0:T(8,128)(2,1)S(1)}, bf16[64,1024]{1,0:T(8,128)(2,1)S(1)}, u32[]{:S(2)}, u32[]{:S(2)}) collective-permute-start(bf16[64,1024]{1,0:T(8,128)(2,1)S(1)} %add.13.refs_0_), channel_id=1, source_target_pairs={{0,12},{1,13},{2,14},{3,15},{4,8},{5,9},{6,10},{7,11},{8,4},{9,5},... | collective-permute-start | bytes 393224 | tf_op jit(solution)/shard_map/ppermute | solution.py:298
  49.0 0.0 collective-permute-start.14
  49.0 1.3 %collective-permute-start.13 = (bf16[64,1024]{1,0:T(8,128)(2,1)S(1)}, bf16[64,1024]{1,0:T(8,128)(2,1)S(1)}, u32[]{:S(2)}, u32[]{:S(2)}) collective-permute-start(bf16[64,1024]{1,0:T(8,128)(2,1)S(1)} %add.13.refs_0_), channel_id=1, source_target_pairs={{0,8},{1,9},{2,10},{3,11},{4,12},{5,13},{6,14},{7,15},{8,0},{9,1},... | collective-permute-start | bytes 393224 | tf_op jit(solution)/shard_map/ppermute | solution.py:298
  50.3 2.7 %collective-permute-done.15.refs_3_ = bf16[64,1024]{1,0:T(8,128)(2,1)S(1)} collective-permute-done((bf16[64,1024]{1,0:T(8,128)(2,1)S(1)}, bf16[64,1024]{1,0:T(8,128)(2,1)S(1)}, u32[]{:S(2)}, u32[]{:S(2)}) %collective-permute-start.15) | collective-permute-done | bytes 131104 | tf_op jit(solution)/shard_map/ppermute | solution.py:298
  53.1 2.6 %collective-permute-done.14.refs_2_ = bf16[64,1024]{1,0:T(8,128)(2,1)S(1)} collective-permute-done((bf16[64,1024]{1,0:T(8,128)(2,1)S(1)}, bf16[64,1024]{1,0:T(8,128)(2,1)S(1)}, u32[]{:S(2)}, u32[]{:S(2)}) %collective-permute-start.14) | collective-permute-done | bytes 131104 | tf_op jit(solution)/shard_map/ppermute | solution.py:298
  55.6 0.6 %collective-permute-done.13.refs_1_ = bf16[64,1024]{1,0:T(8,128)(2,1)S(1)} collective-permute-done((bf16[64,1024]{1,0:T(8,128)(2,1)S(1)}, bf16[64,1024]{1,0:T(8,128)(2,1)S(1)}, u32[]{:S(2)}, u32[]{:S(2)}) %collective-permute-start.13) | collective-permute-done | bytes 131104 | tf_op jit(solution)/shard_map/ppermute | solution.py:298
  56.3 1.6 %to_rows.1 = f32[256,1024]{1,0:T(8,128)} custom-call(s32[2]{0:T(128)S(1)} %pad_add_fusion.info_ref, bf16[64,1024]{1,0:T(8,128)(2,1)S(1)} %add.13.refs_0_, bf16[64,1024]{1,0:T(8,128)(2,1)S(1)} %collective-permute-done.13.refs_1_, bf16[64,1024]{1,0:T(8,128)(2,1)S(1)} %collective-permute-done.14.refs_2_, bf16[64,1024]{1,0:T(8,128)(2,1)S(1)} %collective-permute-done.15.refs_3_), custom_call_target="tpu_custom_call" | custom-call | tf_op jit(solution)/shard_map/to_rows/pallas_call | solution.py:279
  (3 shorter events, 0.1 us)
Async XLA Ops:
  1.7 9.2 %collective-permute-start.3 = (bf16[4,512,512]{2,1,0:T(8,128)(2,1)}, bf16[4,512,512]{2,1,0:T(8,128)(2,1)S(1)}, u32[]{:S(2)}, u32[]{:S(2)}) collective-permute-start(bf16[4,512,512]{2,1,0:T(8,128)(2,1)} %enc_in.1), channel_id=1, source_target_pairs={{0,1},{1,0},{2,3},{3,2},{4,5},{5,4},{6,7},{7,6},{8,9},{9,8},{10,11... | collective-permute-start | bytes 6291464 | tf_op jit(solution)/shard_map/ppermute | solution.py:298
  2.2 15.1 %collective-permute-start.4 = (bf16[2,256,512]{2,1,0:T(8,128)(2,1)S(1)}, bf16[2,256,512]{2,1,0:T(8,128)(2,1)S(1)}, u32[]{:S(2)}, u32[]{:S(2)}) collective-permute-start(bf16[2,256,512]{2,1,0:T(8,128)(2,1)S(1)} %pack.1.qc_ref.refs_2_), channel_id=1, source_target_pairs={{0,2},{1,3},{2,0},{3,1},{4,6},{5,7},{6,4},{7,5},{8,10},{9,11},{10,... | collective-permute-start | bytes 1572872 | tf_op jit(solution)/shard_map/ppermute | solution.py:298
  4.8 6.0 %collective-permute-start = (s32[4]{0:T(128)}, s32[4]{0:T(128)S(1)}, u32[]{:S(2)}, u32[]{:S(2)}) collective-permute-start(s32[4]{0:T(128)} %lens_ref.3), channel_id=1, source_target_pairs={{0,1},{1,0},{2,3},{3,2},{4,5},{5,4},{6,7},{7,6},{8,9},{9,8},{10,11... | collective-permute-start | bytes 56 | tf_op jit(solution)/shard_map/ppermute | solution.py:298
  4.9 5.9 %collective-permute-start.1 = (s32[4,1024]{1,0:T(4,128)}, s32[4,1024]{1,0:T(4,128)S(1)}, u32[]{:S(2)}, u32[]{:S(2)}) collective-permute-start(s32[4,1024]{1,0:T(4,128)} %beam_in.1), channel_id=1, source_target_pairs={{0,1},{1,0},{2,3},{3,2},{4,5},{5,4},{6,7},{7,6},{8,9},{9,8},{10,11... | collective-permute-start | bytes 49160 | tf_op jit(solution)/shard_map/ppermute | solution.py:298
  5.3 5.6 %collective-permute-start.2 = (f32[4,1024]{1,0:T(4,128)}, f32[4,1024]{1,0:T(4,128)S(1)}, u32[]{:S(2)}, u32[]{:S(2)}) collective-permute-start(f32[4,1024]{1,0:T(4,128)} %grad_in.1), channel_id=1, source_target_pairs={{0,1},{1,0},{2,3},{3,2},{4,5},{5,4},{6,7},{7,6},{8,9},{9,8},{10,11... | collective-permute-start | bytes 49160 | tf_op jit(solution)/shard_map/ppermute | solution.py:298
  14.5 9.1 %collective-permute-start.5 = (bf16[128,1024]{1,0:T(8,128)(2,1)S(1)}, bf16[128,1024]{1,0:T(8,128)(2,1)S(1)}, u32[]{:S(2)}, u32[]{:S(2)}) collective-permute-start(bf16[128,1024]{1,0:T(8,128)(2,1)S(1)} %get-tuple-element.77), channel_id=1, source_target_pairs={{0,4},{1,5},{2,6},{3,7},{4,0},{5,1},{6,2},{7,3},{8,12},{9,13},{10,... | collective-permute-start | bytes 786440 | tf_op jit(solution)/shard_map/ppermute | solution.py:298
  23.6 7.3 %collective-permute-start.8 = (bf16[64,1024]{1,0:T(8,128)(2,1)S(1)}, bf16[64,1024]{1,0:T(8,128)(2,1)S(1)}, u32[]{:S(2)}, u32[]{:S(2)}) collective-permute-start(bf16[64,1024]{1,0:T(8,128)(2,1)S(1)} %get-tuple-element.89), channel_id=1, source_target_pairs={{0,4},{1,5},{2,6},{3,7},{4,0},{5,1},{6,2},{7,3},{8,12},{9,13},{10,... | collective-permute-start | bytes 393224 | tf_op jit(solution)/shard_map/ppermute | solution.py:298
  25.5 10.5 %collective-permute-start.6 = (bf16[64,1024]{1,0:T(8,128)(2,1)S(1)}, bf16[64,1024]{1,0:T(8,128)(2,1)S(1)}, u32[]{:S(2)}, u32[]{:S(2)}) collective-permute-start(bf16[64,1024]{1,0:T(8,128)(2,1)S(1)} %get-tuple-element.86), channel_id=1, source_target_pairs={{0,14},{1,15},{2,12},{3,13},{4,10},{5,11},{6,8},{7,9},{8,6},{9,7},... | collective-permute-start | bytes 393224 | tf_op jit(solution)/shard_map/ppermute | solution.py:298
  28.0 8.1 %collective-permute-start.7 = (bf16[64,1024]{1,0:T(8,128)(2,1)S(1)}, bf16[64,1024]{1,0:T(8,128)(2,1)S(1)}, u32[]{:S(2)}, u32[]{:S(2)}) collective-permute-start(bf16[64,1024]{1,0:T(8,128)(2,1)S(1)} %get-tuple-element.87), channel_id=1, source_target_pairs={{0,10},{1,11},{2,8},{3,9},{4,14},{5,15},{6,12},{7,13},{8,2},{9,3},... | collective-permute-start | bytes 393224 | tf_op jit(solution)/shard_map/ppermute | solution.py:298
  31.0 5.8 %collective-permute-start.9 = (bf16[64,1024]{1,0:T(8,128)(2,1)S(1)}, bf16[64,1024]{1,0:T(8,128)(2,1)S(1)}, u32[]{:S(2)}, u32[]{:S(2)}) collective-permute-start(bf16[64,1024]{1,0:T(8,128)(2,1)S(1)} %add.11), channel_id=1, source_target_pairs={{0,2},{1,3},{2,0},{3,1},{4,6},{5,7},{6,4},{7,5},{8,10},{9,11},{10,... | collective-permute-start | bytes 393224 | tf_op jit(solution)/shard_map/ppermute | solution.py:298
  31.4 5.5 %collective-permute-start.10 = (bf16[64,1024]{1,0:T(8,128)(2,1)S(1)}, bf16[64,1024]{1,0:T(8,128)(2,1)S(1)}, u32[]{:S(2)}, u32[]{:S(2)}) collective-permute-start(bf16[64,1024]{1,0:T(8,128)(2,1)S(1)} %get-tuple-element.99), channel_id=1, source_target_pairs={{0,8},{1,9},{2,10},{3,11},{4,12},{5,13},{6,14},{7,15},{8,0},{9,1},... | collective-permute-start | bytes 393224 | tf_op jit(solution)/shard_map/ppermute | solution.py:298
  36.9 4.3 %collective-permute-start.11 = (bf16[4,528,512]{2,1,0:T(8,128)(2,1)S(1)}, bf16[4,528,512]{2,1,0:T(8,128)(2,1)S(1)}, u32[]{:S(2)}, u32[]{:S(2)}) collective-permute-start(bf16[4,528,512]{2,1,0:T(8,128)(2,1)S(1)} %state_away.1), channel_id=1, source_target_pairs={{0,1},{1,0},{2,3},{3,2},{4,5},{5,4},{6,7},{7,6},{8,9},{9,8},{10,11... | collective-permute-start | bytes 6488072 | tf_op jit(solution)/shard_map/ppermute | solution.py:298
  37.0 9.7 %collective-permute-start.12 = (bf16[64,1024]{1,0:T(8,128)(2,1)S(1)}, bf16[64,1024]{1,0:T(8,128)(2,1)S(1)}, u32[]{:S(2)}, u32[]{:S(2)}) collective-permute-start(bf16[64,1024]{1,0:T(8,128)(2,1)S(1)} %add.12.refs_0_), channel_id=1, source_target_pairs={{0,16},{1,17},{2,18},{3,19},{4,20},{5,21},{6,22},{7,23},{8,24},{9,... | collective-permute-start | bytes 393224 | tf_op jit(solution)/shard_map/ppermute | solution.py:298
  46.7 6.3 %collective-permute-start.15 = (bf16[64,1024]{1,0:T(8,128)(2,1)S(1)}, bf16[64,1024]{1,0:T(8,128)(2,1)S(1)}, u32[]{:S(2)}, u32[]{:S(2)}) collective-permute-start(bf16[64,1024]{1,0:T(8,128)(2,1)S(1)} %add.13.refs_0_), channel_id=1, source_target_pairs={{0,12},{1,13},{2,14},{3,15},{4,8},{5,9},{6,10},{7,11},{8,4},{9,5},... | collective-permute-start | bytes 393224 | tf_op jit(solution)/shard_map/ppermute | solution.py:298
  49.0 6.7 %collective-permute-start.14 = (bf16[64,1024]{1,0:T(8,128)(2,1)S(1)}, bf16[64,1024]{1,0:T(8,128)(2,1)S(1)}, u32[]{:S(2)}, u32[]{:S(2)}) collective-permute-start(bf16[64,1024]{1,0:T(8,128)(2,1)S(1)} %add.13.refs_0_), channel_id=1, source_target_pairs={{0,4},{1,5},{2,6},{3,7},{4,0},{5,1},{6,2},{7,3},{8,12},{9,13},{10,... | collective-permute-start | bytes 393224 | tf_op jit(solution)/shard_map/ppermute | solution.py:298
  49.0 7.3 %collective-permute-start.13 = (bf16[64,1024]{1,0:T(8,128)(2,1)S(1)}, bf16[64,1024]{1,0:T(8,128)(2,1)S(1)}, u32[]{:S(2)}, u32[]{:S(2)}) collective-permute-start(bf16[64,1024]{1,0:T(8,128)(2,1)S(1)} %add.13.refs_0_), channel_id=1, source_target_pairs={{0,8},{1,9},{2,10},{3,11},{4,12},{5,13},{6,14},{7,15},{8,0},{9,1},... | collective-permute-start | bytes 393224 | tf_op jit(solution)/shard_map/ppermute | solution.py:298
where the time goes:
time: 58.2 us; the launch traced here: 58 us
  Pallas kernels  25.6 us (44%)
  starting transfers between devices  18.2 us (31%)
  waiting for transfers between devices  13.2 us (23%)
  between operations  0.92 us (2%)
    pallas_call x9, Pallas kernels, call(): pl.pallas_call(kernel, out_shape=out_shape, in_specs=[HBM if i < hbm else...  19.5 us
    ppermute x16, starting transfers between devices, swap(): lax.ppermute(x, ('rep', 'blk'), [(i, i ^ mask) for i in range(total)])  18.2 us
    ppermute x16, waiting for transfers between devices, swap(): lax.ppermute(x, ('rep', 'blk'), [(i, i ^ mask) for i in range(total)])  13.2 us
    pallas_call x1, Pallas kernels, state_grad(): pl.pallas_call(functools.partial(home_kernel, (0, 2)), out_shape=[out, sh...  4.55 us
    pallas_call x1, Pallas kernels, to_rows(): pl.pallas_call(rows_kernel, out_shape=shape((count * rows, cols), F32), i...  1.55 us
  transfers between devices with their start and end apart: 16, of which 9 were waited for; matrix products, arithmetic and copies ran while one was open for 0% of the time, Pallas kernels for 39%

commit v1 on v0

--- a/solution.py
+++ b/solution.py
@@ -15,6 +15,9 @@
 PARAMS = pltpu.CompilerParams(vmem_limit_bytes=20 * 1024 * 1024)
 GROUP = 4
 EXTRA = 16
+
+
+LONG = pl.CostEstimate(flops=10**11, transcendentals=0, bytes_accessed=0)
 
 
 def shape(dims, dtype):
@@ -254,10 +257,12 @@
         ref[...] = total[i * size : (i + 1) * size].astype(ref.dtype)
 
 
-def add(arrays, dtypes):
+def add(arrays, dtypes, estimate=None):
     rows, cols = arrays[0].shape
     out = [shape((rows // len(dtypes), cols), dtype) for dtype in dtypes]
-    return call(functools.partial(add_kernel, len(arrays)), out, arrays, "add")
+    return call(
+        functools.partial(add_kernel, len(arrays)), out, arrays, "add", estimate=estimate
+    )
 
 
 def rows_kernel(info_ref, *refs):
@@ -356,9 +361,9 @@
         info, gate2,
         [(attn2, score2, qc, logit2), (far_attn2, far_score2, far_qc, far_logit2)], [],
     )
-    received, state2, near = lax.optimization_barrier((received, state2, near))
+    received, near = lax.optimization_barrier((received, near))
     state_in = swap(state2, core)
-    (own,) = add([keep, near, *received], [BF16])
+    (own,) = add([keep, near, *received], [BF16], LONG)
     far_attn, far_score, own = lax.optimization_barrier((far_attn, far_score, own))
     state, logits = state_grad(
         info, gate, [(attn, score, qc, logit), (far_attn, far_score, far_qc, far_logit)],

time: 58.2 us -> 58.1 us (level)
  no operation moved by 1% of the time
where the time goes in v1:
time: 58.1 us; the launch traced here: 58 us
  Pallas kernels  25.6 us (44%)
  starting transfers between devices  18.7 us (32%)
  waiting for transfers between devices  12.7 us (22%)
  between operations  0.93 us (2%)
    pallas_call x9, Pallas kernels, call(): pl.pallas_call(kernel, out_shape=out_shape, in_specs=[HBM if i < hbm else...  19.5 us
    ppermute x16, starting transfers between devices, swap(): lax.ppermute(x, ('rep', 'blk'), [(i, i ^ mask) for i in range(total)])  18.7 us
    ppermute x16, waiting for transfers between devices, swap(): lax.ppermute(x, ('rep', 'blk'), [(i, i ^ mask) for i in range(total)])  12.7 us
    pallas_call x1, Pallas kernels, state_grad(): pl.pallas_call(functools.partial(home_kernel, (0, 2)), out_shape=[out, sh...  4.55 us
    pallas_call x1, Pallas kernels, to_rows(): pl.pallas_call(rows_kernel, out_shape=shape((count * rows, cols), F32), i...  1.55 us
  transfers between devices with their start and end apart: 16, of which 9 were waited for; matrix products, arithmetic and copies ran while one was open for 0% of the time, Pallas kernels for 39%

profile of v1, /device:TPU:0, one launch (start us, length us, event | category | flops | bytes accessed | tf_op | source)
XLA Modules:
  0.0 58.0 jit_solution(1344978514396692945)
XLA Ops:
  0.6 1.0 %pack.1.qc_ref.refs_2_ = bf16[2,256,512]{2,1,0:T(8,128)(2,1)S(1)} custom-call(bf16[256,512]{1,0:T(8,128)(2,1)} %q_in.1, bf16[256,512]{1,0:T(8,128)(2,1)} %c_in.1), custom_call_target="tpu_custom_call" | custom-call | tf_op jit(solution)/shard_map/pack/pallas_call | solution.py:42
  1.7 0.5 collective-permute-start.3
  2.2 2.6 %collective-permute-start.4 = (bf16[2,256,512]{2,1,0:T(8,128)(2,1)S(1)}, bf16[2,256,512]{2,1,0:T(8,128)(2,1)S(1)}, u32[]{:S(2)}, u32[]{:S(2)}) collective-permute-start(bf16[2,256,512]{2,1,0:T(8,128)(2,1)S(1)} %pack.1.qc_ref.refs_2_), channel_id=1, source_target_pairs={{0,2},{1,3},{2,0},{3,1},{4,6},{5,7},{6,4},{7,5},{8,10},{9,11},{10,... | collective-permute-start | bytes 1572872 | tf_op jit(solution)/shard_map/ppermute | solution.py:303
  4.8 0.2 collective-permute-start
  4.9 0.3 collective-permute-start.1
  5.3 0.2 collective-permute-start.2
  5.4 0.1 pad_add_fusion.info_ref
  5.5 5.3 %own_labels.1 = (bf16[4,512,512]{2,1,0:T(8,128)(2,1)S(1)}, f32[4,1024]{1,0:T(4,128)S(1)}, bf16[4,512,512]{2,1,0:T(8,128)(2,1)S(1)}, bf16[4,512,256]{2,1,0:T(8,12...) custom-call(bf16[4,512,512]{2,1,0:T(8,128)(2,1)} %enc_in.1, ...), custom_call_target="tpu_custom_call" | custom-call | flops 2147483648 | bytes 4194304 | tf_op jit(solution)/shard_map/own_labels/pallas_call | solution.py:42
  10.8 0.0 collective-permute-done.lens_ref.lens2_ref
  10.8 0.0 collective-permute-done.1.beam_ref
  10.8 0.0 collective-permute-done.2.grad_ref
  10.8 0.0 collective-permute-done.3.enc_ref.enc2_ref
  10.9 3.6 %own_labels_other_docs.1 = (f32[4,1024]{1,0:T(4,128)S(1)}, bf16[4,512,512]{2,1,0:T(8,128)(2,1)S(1)}, bf16[4,512,256]{2,1,0:T(8,128)(2,1)S(1)}, bf16[4,512,256]{2...) custom-call(s32[2]{0:T(128)S(1)} %pad_add_fusion.info_ref, ...), custom_call_target="tpu_custom_call" | custom-call | flops 2147483648 | bytes 4194304 | tf_op jit(solution)/shard_map/own_labels_other_docs/pallas_call | solution.py:42
  14.4 1.6 %collective-permute-start.5 = (bf16[128,1024]{1,0:T(8,128)(2,1)S(1)}, bf16[128,1024]{1,0:T(8,128)(2,1)S(1)}, u32[]{:S(2)}, u32[]{:S(2)}) collective-permute-start(bf16[128,1024]{1,0:T(8,128)(2,1)S(1)} %get-tuple-element.76), channel_id=1, source_target_pairs={{0,4},{1,5},{2,6},{3,7},{4,0},{5,1},{6,2},{7,3},{8,12},{9,13},{10,... | collective-permute-start | bytes 786440 | tf_op jit(solution)/shard_map/ppermute | solution.py:303
  16.0 1.3 %collective-permute-done.4.qc_ref.refs_6_ = bf16[2,256,512]{2,1,0:T(8,128)(2,1)S(1)} collective-permute-done((bf16[2,256,512]{2,1,0:T(8,128)(2,1)S(1)}, bf16[2,256,512]{2,1,0:T(8,128)(2,1)S(1)}, u32[]{:S(2)}, u32[]{:S(2)}) %collective-permute-start.4) | collective-permute-done | bytes 524320 | tf_op jit(solution)/shard_map/ppermute | solution.py:303
  17.3 6.3 %far_labels.1 = (bf16[4,512,256]{2,1,0:T(8,128)(2,1)S(1)}, bf16[4,512,256]{2,1,0:T(8,128)(2,1)S(1)}, f32[4,256]{1,0:T(4,128)S(1)}, bf16[4,512,256]{2,1,0:T(8,128...) custom-call(s32[2]{0:T(128)S(1)} %pad_add_fusion.info_ref, ...), custom_call_target="tpu_custom_call" | custom-call | flops 4294967296 | bytes 8388608 | tf_op jit(solution)/shard_map/far_labels/pallas_call | solution.py:42
  23.6 0.0 collective-permute-done.5.refs_1_
  23.7 1.9 %collective-permute-start.8 = (bf16[64,1024]{1,0:T(8,128)(2,1)S(1)}, bf16[64,1024]{1,0:T(8,128)(2,1)S(1)}, u32[]{:S(2)}, u32[]{:S(2)}) collective-permute-start(bf16[64,1024]{1,0:T(8,128)(2,1)S(1)} %get-tuple-element.88), channel_id=1, source_target_pairs={{0,4},{1,5},{2,6},{3,7},{4,0},{5,1},{6,2},{7,3},{8,12},{9,13},{10,... | collective-permute-start | bytes 393224 | tf_op jit(solution)/shard_map/ppermute | solution.py:303
  25.5 2.4 %collective-permute-start.6 = (bf16[64,1024]{1,0:T(8,128)(2,1)S(1)}, bf16[64,1024]{1,0:T(8,128)(2,1)S(1)}, u32[]{:S(2)}, u32[]{:S(2)}) collective-permute-start(bf16[64,1024]{1,0:T(8,128)(2,1)S(1)} %get-tuple-element.85), channel_id=1, source_target_pairs={{0,14},{1,15},{2,12},{3,13},{4,10},{5,11},{6,8},{7,9},{8,6},{9,7},... | collective-permute-start | bytes 393224 | tf_op jit(solution)/shard_map/ppermute | solution.py:303
  28.0 0.2 collective-permute-start.7
  28.1 2.8 %collective-permute-done.8.refs_1_ = bf16[64,1024]{1,0:T(8,128)(2,1)S(1)} collective-permute-done((bf16[64,1024]{1,0:T(8,128)(2,1)S(1)}, bf16[64,1024]{1,0:T(8,128)(2,1)S(1)}, u32[]{:S(2)}, u32[]{:S(2)}) %collective-permute-start.8) | collective-permute-done | bytes 131104 | tf_op jit(solution)/shard_map/ppermute | solution.py:303
  30.9 0.5 collective-permute-start.9
  31.4 1.6 %collective-permute-start.10 = (bf16[64,1024]{1,0:T(8,128)(2,1)S(1)}, bf16[64,1024]{1,0:T(8,128)(2,1)S(1)}, u32[]{:S(2)}, u32[]{:S(2)}) collective-permute-start(bf16[64,1024]{1,0:T(8,128)(2,1)S(1)} %get-tuple-element.92), channel_id=1, source_target_pairs={{0,8},{1,9},{2,10},{3,11},{4,12},{5,13},{6,14},{7,15},{8,0},{9,1},... | collective-permute-start | bytes 393224 | tf_op jit(solution)/shard_map/ppermute | solution.py:303
  33.0 3.1 %state_away.1 = bf16[4,528,512]{2,1,0:T(8,128)(2,1)S(1)} custom-call(s32[2]{0:T(128)S(1)} %pad_add_fusion.info_ref, f32[4,1024]{1,0:T(4,128)S(1)} %get-tuple-element.65.gate2_ref.gate_ref, bf16[4,512,256]{2,1,0:T(8,128)(2,1)S(1)} %get-tuple-element.100.refs_0_, bf16[4,512,256]{2,1,0:T(8,128)(2,1)S(1)} %get-tuple-element.101.refs_1_, ...), custom_call_target="tpu_custom_call" | custom-call | flops 2147483648 | bytes 4194304 | tf_op jit(solution)/shard_map/state_away/pallas_call | solution.py:42
  36.1 0.1 collective-permute-start.11
  36.1 0.0 collective-permute-done.6.refs_2_
  36.1 0.0 collective-permute-done.7.refs_3_
  36.2 0.6 collective-permute-done.9.refs_4_
  36.7 0.1 collective-permute-done.10.refs_1_
  36.9 0.1 add.12.refs_0_
  37.0 2.7 %collective-permute-start.12 = (bf16[64,1024]{1,0:T(8,128)(2,1)S(1)}, bf16[64,1024]{1,0:T(8,128)(2,1)S(1)}, u32[]{:S(2)}, u32[]{:S(2)}) collective-permute-start(bf16[64,1024]{1,0:T(8,128)(2,1)S(1)} %add.12.refs_0_), channel_id=1, source_target_pairs={{0,16},{1,17},{2,18},{3,19},{4,20},{5,21},{6,22},{7,23},{8,24},{9,... | collective-permute-start | bytes 393224 | tf_op jit(solution)/shard_map/ppermute | solution.py:303
  39.7 0.7 %collective-permute-done.11.refs_8_ = bf16[4,528,512]{2,1,0:T(8,128)(2,1)S(1)} collective-permute-done((bf16[4,528,512]{2,1,0:T(8,128)(2,1)S(1)}, bf16[4,528,512]{2,1,0:T(8,128)(2,1)S(1)}, u32[]{:S(2)}, u32[]{:S(2)}) %collective-permute-start.11) | collective-permute-done | bytes 2162720 | tf_op jit(solution)/shard_map/ppermute | solution.py:303
  40.4 4.6 %state_home.1 = (bf16[4,512,512]{2,1,0:T(8,128)(2,1)}, f32[4,1024]{1,0:T(4,128)}) custom-call(s32[2]{0:T(128)S(1)} %pad_add_fusion.info_ref, f32[4,1024]{1,0:T(4,128)S(1)} %get-tuple-element.58.gate_ref, bf16[4,512,256]{2,1,0:T(8,128)(2,1)S(1)} %get-tuple-element.59.refs_0_, bf16[4,512,256]{2,1,0:T(8,128)(2,1)S(1)} %get-tuple-element.60.refs_1_, ...), custom_call_target="tpu_custom_call" | custom-call | flops 2147483648 | bytes 4194304 | tf_op jit(solution)/shard_map/state_home/pallas_call | solution.py:239
  44.9 1.0 %collective-permute-done.12.refs_1_ = bf16[64,1024]{1,0:T(8,128)(2,1)S(1)} collective-permute-done((bf16[64,1024]{1,0:T(8,128)(2,1)S(1)}, bf16[64,1024]{1,0:T(8,128)(2,1)S(1)}, u32[]{:S(2)}, u32[]{:S(2)}) %collective-permute-start.12) | collective-permute-done | bytes 131104 | tf_op jit(solution)/shard_map/ppermute | solution.py:303
  46.0 1.7 %collective-permute-start.15 = (bf16[64,1024]{1,0:T(8,128)(2,1)S(1)}, bf16[64,1024]{1,0:T(8,128)(2,1)S(1)}, u32[]{:S(2)}, u32[]{:S(2)}) collective-permute-start(bf16[64,1024]{1,0:T(8,128)(2,1)S(1)} %add.13.refs_0_), channel_id=1, source_target_pairs={{0,12},{1,13},{2,14},{3,15},{4,8},{5,9},{6,10},{7,11},{8,4},{9,5},... | collective-permute-start | bytes 393224 | tf_op jit(solution)/shard_map/ppermute | solution.py:303
  47.7 0.9 %collective-permute-start.14 = (bf16[64,1024]{1,0:T(8,128)(2,1)S(1)}, bf16[64,1024]{1,0:T(8,128)(2,1)S(1)}, u32[]{:S(2)}, u32[]{:S(2)}) collective-permute-start(bf16[64,1024]{1,0:T(8,128)(2,1)S(1)} %add.13.refs_0_), channel_id=1, source_target_pairs={{0,4},{1,5},{2,6},{3,7},{4,0},{5,1},{6,2},{7,3},{8,12},{9,13},{10,... | collective-permute-start | bytes 393224 | tf_op jit(solution)/shard_map/ppermute | solution.py:303
  48.6 1.4 %collective-permute-start.13 = (bf16[64,1024]{1,0:T(8,128)(2,1)S(1)}, bf16[64,1024]{1,0:T(8,128)(2,1)S(1)}, u32[]{:S(2)}, u32[]{:S(2)}) collective-permute-start(bf16[64,1024]{1,0:T(8,128)(2,1)S(1)} %add.13.refs_0_), channel_id=1, source_target_pairs={{0,8},{1,9},{2,10},{3,11},{4,12},{5,13},{6,14},{7,15},{8,0},{9,1},... | collective-permute-start | bytes 393224 | tf_op jit(solution)/shard_map/ppermute | solution.py:303
  50.0 2.0 %collective-permute-done.15.refs_3_ = bf16[64,1024]{1,0:T(8,128)(2,1)S(1)} collective-permute-done((bf16[64,1024]{1,0:T(8,128)(2,1)S(1)}, bf16[64,1024]{1,0:T(8,128)(2,1)S(1)}, u32[]{:S(2)}, u32[]{:S(2)}) %collective-permute-start.15) | collective-permute-done | bytes 131104 | tf_op jit(solution)/shard_map/ppermute | solution.py:303
  52.0 2.5 %collective-permute-done.14.refs_2_ = bf16[64,1024]{1,0:T(8,128)(2,1)S(1)} collective-permute-done((bf16[64,1024]{1,0:T(8,128)(2,1)S(1)}, bf16[64,1024]{1,0:T(8,128)(2,1)S(1)}, u32[]{:S(2)}, u32[]{:S(2)}) %collective-permute-start.14) | collective-permute-done | bytes 131104 | tf_op jit(solution)/shard_map/ppermute | solution.py:303
  54.5 1.7 %collective-permute-done.13.refs_1_ = bf16[64,1024]{1,0:T(8,128)(2,1)S(1)} collective-permute-done((bf16[64,1024]{1,0:T(8,128)(2,1)S(1)}, bf16[64,1024]{1,0:T(8,128)(2,1)S(1)}, u32[]{:S(2)}, u32[]{:S(2)}) %collective-permute-start.13) | collective-permute-done | bytes 131104 | tf_op jit(solution)/shard_map/ppermute | solution.py:303
  56.2 1.6 %to_rows.1 = f32[256,1024]{1,0:T(8,128)} custom-call(s32[2]{0:T(128)S(1)} %pad_add_fusion.info_ref, bf16[64,1024]{1,0:T(8,128)(2,1)S(1)} %add.13.refs_0_, bf16[64,1024]{1,0:T(8,128)(2,1)S(1)} %collective-permute-done.13.refs_1_, bf16[64,1024]{1,0:T(8,128)(2,1)S(1)} %collective-permute-done.14.refs_2_, bf16[64,1024]{1,0:T(8,128)(2,1)S(1)} %collective-permute-done.15.refs_3_), custom_call_target="tpu_custom_call" | custom-call | tf_op jit(solution)/shard_map/to_rows/pallas_call | solution.py:284
  (3 shorter events, 0.1 us)
Async XLA Ops:
  1.7 9.2 %collective-permute-start.3 = (bf16[4,512,512]{2,1,0:T(8,128)(2,1)}, bf16[4,512,512]{2,1,0:T(8,128)(2,1)S(1)}, u32[]{:S(2)}, u32[]{:S(2)}) collective-permute-start(bf16[4,512,512]{2,1,0:T(8,128)(2,1)} %enc_in.1), channel_id=1, source_target_pairs={{0,1},{1,0},{2,3},{3,2},{4,5},{5,4},{6,7},{7,6},{8,9},{9,8},{10,11... | collective-permute-start | bytes 6291464 | tf_op jit(solution)/shard_map/ppermute | solution.py:303
  2.2 15.1 %collective-permute-start.4 = (bf16[2,256,512]{2,1,0:T(8,128)(2,1)S(1)}, bf16[2,256,512]{2,1,0:T(8,128)(2,1)S(1)}, u32[]{:S(2)}, u32[]{:S(2)}) collective-permute-start(bf16[2,256,512]{2,1,0:T(8,128)(2,1)S(1)} %pack.1.qc_ref.refs_2_), channel_id=1, source_target_pairs={{0,2},{1,3},{2,0},{3,1},{4,6},{5,7},{6,4},{7,5},{8,10},{9,11},{10,... | collective-permute-start | bytes 1572872 | tf_op jit(solution)/shard_map/ppermute | solution.py:303
  4.8 6.0 %collective-permute-start = (s32[4]{0:T(128)}, s32[4]{0:T(128)S(1)}, u32[]{:S(2)}, u32[]{:S(2)}) collective-permute-start(s32[4]{0:T(128)} %lens_ref.3), channel_id=1, source_target_pairs={{0,1},{1,0},{2,3},{3,2},{4,5},{5,4},{6,7},{7,6},{8,9},{9,8},{10,11... | collective-permute-start | bytes 56 | tf_op jit(solution)/shard_map/ppermute | solution.py:303
  4.9 5.9 %collective-permute-start.1 = (s32[4,1024]{1,0:T(4,128)}, s32[4,1024]{1,0:T(4,128)S(1)}, u32[]{:S(2)}, u32[]{:S(2)}) collective-permute-start(s32[4,1024]{1,0:T(4,128)} %beam_in.1), channel_id=1, source_target_pairs={{0,1},{1,0},{2,3},{3,2},{4,5},{5,4},{6,7},{7,6},{8,9},{9,8},{10,11... | collective-permute-start | bytes 49160 | tf_op jit(solution)/shard_map/ppermute | solution.py:303
  5.3 5.6 %collective-permute-start.2 = (f32[4,1024]{1,0:T(4,128)}, f32[4,1024]{1,0:T(4,128)S(1)}, u32[]{:S(2)}, u32[]{:S(2)}) collective-permute-start(f32[4,1024]{1,0:T(4,128)} %grad_in.1), channel_id=1, source_target_pairs={{0,1},{1,0},{2,3},{3,2},{4,5},{5,4},{6,7},{7,6},{8,9},{9,8},{10,11... | collective-permute-start | bytes 49160 | tf_op jit(solution)/shard_map/ppermute | solution.py:303
  14.4 9.1 %collective-permute-start.5 = (bf16[128,1024]{1,0:T(8,128)(2,1)S(1)}, bf16[128,1024]{1,0:T(8,128)(2,1)S(1)}, u32[]{:S(2)}, u32[]{:S(2)}) collective-permute-start(bf16[128,1024]{1,0:T(8,128)(2,1)S(1)} %get-tuple-element.76), channel_id=1, source_target_pairs={{0,4},{1,5},{2,6},{3,7},{4,0},{5,1},{6,2},{7,3},{8,12},{9,13},{10,... | collective-permute-start | bytes 786440 | tf_op jit(solution)/shard_map/ppermute | solution.py:303
  23.7 7.3 %collective-permute-start.8 = (bf16[64,1024]{1,0:T(8,128)(2,1)S(1)}, bf16[64,1024]{1,0:T(8,128)(2,1)S(1)}, u32[]{:S(2)}, u32[]{:S(2)}) collective-permute-start(bf16[64,1024]{1,0:T(8,128)(2,1)S(1)} %get-tuple-element.88), channel_id=1, source_target_pairs={{0,4},{1,5},{2,6},{3,7},{4,0},{5,1},{6,2},{7,3},{8,12},{9,13},{10,... | collective-permute-start | bytes 393224 | tf_op jit(solution)/shard_map/ppermute | solution.py:303
  25.5 10.6 %collective-permute-start.6 = (bf16[64,1024]{1,0:T(8,128)(2,1)S(1)}, bf16[64,1024]{1,0:T(8,128)(2,1)S(1)}, u32[]{:S(2)}, u32[]{:S(2)}) collective-permute-start(bf16[64,1024]{1,0:T(8,128)(2,1)S(1)} %get-tuple-element.85), channel_id=1, source_target_pairs={{0,14},{1,15},{2,12},{3,13},{4,10},{5,11},{6,8},{7,9},{8,6},{9,7},... | collective-permute-start | bytes 393224 | tf_op jit(solution)/shard_map/ppermute | solution.py:303
  28.0 8.2 %collective-permute-start.7 = (bf16[64,1024]{1,0:T(8,128)(2,1)S(1)}, bf16[64,1024]{1,0:T(8,128)(2,1)S(1)}, u32[]{:S(2)}, u32[]{:S(2)}) collective-permute-start(bf16[64,1024]{1,0:T(8,128)(2,1)S(1)} %get-tuple-element.86), channel_id=1, source_target_pairs={{0,10},{1,11},{2,8},{3,9},{4,14},{5,15},{6,12},{7,13},{8,2},{9,3},... | collective-permute-start | bytes 393224 | tf_op jit(solution)/shard_map/ppermute | solution.py:303
  30.9 5.8 %collective-permute-start.9 = (bf16[64,1024]{1,0:T(8,128)(2,1)S(1)}, bf16[64,1024]{1,0:T(8,128)(2,1)S(1)}, u32[]{:S(2)}, u32[]{:S(2)}) collective-permute-start(bf16[64,1024]{1,0:T(8,128)(2,1)S(1)} %add.11), channel_id=1, source_target_pairs={{0,2},{1,3},{2,0},{3,1},{4,6},{5,7},{6,4},{7,5},{8,10},{9,11},{10,... | collective-permute-start | bytes 393224 | tf_op jit(solution)/shard_map/ppermute | solution.py:303
  31.4 5.4 %collective-permute-start.10 = (bf16[64,1024]{1,0:T(8,128)(2,1)S(1)}, bf16[64,1024]{1,0:T(8,128)(2,1)S(1)}, u32[]{:S(2)}, u32[]{:S(2)}) collective-permute-start(bf16[64,1024]{1,0:T(8,128)(2,1)S(1)} %get-tuple-element.92), channel_id=1, source_target_pairs={{0,8},{1,9},{2,10},{3,11},{4,12},{5,13},{6,14},{7,15},{8,0},{9,1},... | collective-permute-start | bytes 393224 | tf_op jit(solution)/shard_map/ppermute | solution.py:303
  36.1 4.3 %collective-permute-start.11 = (bf16[4,528,512]{2,1,0:T(8,128)(2,1)S(1)}, bf16[4,528,512]{2,1,0:T(8,128)(2,1)S(1)}, u32[]{:S(2)}, u32[]{:S(2)}) collective-permute-start(bf16[4,528,512]{2,1,0:T(8,128)(2,1)S(1)} %state_away.1), channel_id=1, source_target_pairs={{0,1},{1,0},{2,3},{3,2},{4,5},{5,4},{6,7},{7,6},{8,9},{9,8},{10,11... | collective-permute-start | bytes 6488072 | tf_op jit(solution)/shard_map/ppermute | solution.py:303
  37.0 9.0 %collective-permute-start.12 = (bf16[64,1024]{1,0:T(8,128)(2,1)S(1)}, bf16[64,1024]{1,0:T(8,128)(2,1)S(1)}, u32[]{:S(2)}, u32[]{:S(2)}) collective-permute-start(bf16[64,1024]{1,0:T(8,128)(2,1)S(1)} %add.12.refs_0_), channel_id=1, source_target_pairs={{0,16},{1,17},{2,18},{3,19},{4,20},{5,21},{6,22},{7,23},{8,24},{9,... | collective-permute-start | bytes 393224 | tf_op jit(solution)/shard_map/ppermute | solution.py:303
  46.0 6.0 %collective-permute-start.15 = (bf16[64,1024]{1,0:T(8,128)(2,1)S(1)}, bf16[64,1024]{1,0:T(8,128)(2,1)S(1)}, u32[]{:S(2)}, u32[]{:S(2)}) collective-permute-start(bf16[64,1024]{1,0:T(8,128)(2,1)S(1)} %add.13.refs_0_), channel_id=1, source_target_pairs={{0,12},{1,13},{2,14},{3,15},{4,8},{5,9},{6,10},{7,11},{8,4},{9,5},... | collective-permute-start | bytes 393224 | tf_op jit(solution)/shard_map/ppermute | solution.py:303
  47.7 6.8 %collective-permute-start.14 = (bf16[64,1024]{1,0:T(8,128)(2,1)S(1)}, bf16[64,1024]{1,0:T(8,128)(2,1)S(1)}, u32[]{:S(2)}, u32[]{:S(2)}) collective-permute-start(bf16[64,1024]{1,0:T(8,128)(2,1)S(1)} %add.13.refs_0_), channel_id=1, source_target_pairs={{0,4},{1,5},{2,6},{3,7},{4,0},{5,1},{6,2},{7,3},{8,12},{9,13},{10,... | collective-permute-start | bytes 393224 | tf_op jit(solution)/shard_map/ppermute | solution.py:303
  48.6 7.7 %collective-permute-start.13 = (bf16[64,1024]{1,0:T(8,128)(2,1)S(1)}, bf16[64,1024]{1,0:T(8,128)(2,1)S(1)}, u32[]{:S(2)}, u32[]{:S(2)}) collective-permute-start(bf16[64,1024]{1,0:T(8,128)(2,1)S(1)} %add.13.refs_0_), channel_id=1, source_target_pairs={{0,8},{1,9},{2,10},{3,11},{4,12},{5,13},{6,14},{7,15},{8,0},{9,1},... | collective-permute-start | bytes 393224 | tf_op jit(solution)/shard_map/ppermute | solution.py:303
